TPU v7x, 256 devices: a whole 4x4x8 slice. The times are simulated.
256 devices in a mesh: grp: 8 (over y, x_hi), blk: 32 (over x_lo, z, core).
Axes of the slice: x: 4 (x_hi: 2, x_lo: 2; x = x_hi * 2 + x_lo), y: 4, z: 8, core: 2. Of those that a mesh axis runs over, the one named last changes fastest.
Arguments:
- large_emb: bfloat16 [98304, 768], P(('grp', 'blk'))
- large_count: int32 [8], P('grp'), may hold values from 6144 to 12288, as said below
- small_emb: bfloat16 [8, 32, 512, 768], P('grp', 'blk')
- small_ids: int32 [8, 32], P('grp', 'blk'), may hold values from 0 to 7
- small_count: int32 [8, 32], P('grp', 'blk'), may hold values from 128 to 512, as said below
Outputs:
- large_max: float32 [98304], P(('grp', 'blk'))
- small_max: float32 [8, 32, 512], P('grp', 'blk')
Inputs may be any that keep to these rules, and one draw needn't show every extreme that they name: `large_count`: the live rows of a large cluster are its first rows; at least one cluster is fully live in every draw. `small_count`: the live rows of a block are its first rows; at least one block is fully live in every draw. `small_ids`: ids only matter within one column; equal ids in a column mean one cluster.
All inputs are finite; a program needn't handle non-finite values.
Results may differ from a plain program's by a relative error of at most 0.00059.
Values may be sent and summed in bfloat16 or wider, within the bound.
A program may use at most 128 MiB of HBM per device.

v0:
```python
import jax
import jax.numpy as jnp
from jax import lax
from jax.sharding import PartitionSpec as P

EPSILON = 1e-06


def unit_rows(embedding):
    widened = embedding.astype(jnp.float32)
    inverse = lax.rsqrt(jnp.sum(widened * widened, axis=-1, keepdims=True) + EPSILON)
    return (widened * inverse).astype(jnp.bfloat16)


def masked_scores(queries, query_pos, keys, key_pos, live_count):
    scores = jnp.einsum("qd,kd->qk", queries, keys, preferred_element_type=jnp.float32)
    valid = (
        (query_pos[:, None] < live_count)
        & (key_pos[None, :] < live_count)
        & (query_pos[:, None] != key_pos[None, :])
    )
    return jnp.where(valid, scores, -2.0)


def body(large_emb, large_count, small_emb, small_ids, small_count):
    local_rows = unit_rows(large_emb)
    rows_dev = local_rows.shape[0]
    own_shard = lax.axis_index("blk")
    positions = own_shard * rows_dev + jnp.arange(rows_dev, dtype=jnp.int32)
    live_count = large_count[0]
    start_best = jnp.full((rows_dev,), -1.0, jnp.float32)
    piece = lax.all_gather(local_rows, "blk", axis=0, tiled=True)
    total = piece.shape[0]
    width = 512

    def visit_keys(offset, current):
        first = offset * width
        keys = lax.dynamic_slice_in_dim(piece, first, width, 0)
        key_pos = first + jnp.arange(width, dtype=jnp.int32)

        def compute(previous):
            scores = masked_scores(local_rows, positions, keys, key_pos, live_count)
            return jnp.maximum(previous, jnp.max(scores, axis=1))

        return compute(current)

    best_sim = lax.fori_loop(0, total // width, visit_keys, start_best)
    large_max = jnp.where(positions < live_count, best_sim, 0.0)
    small_rows = unit_rows(small_emb)[:, 0]
    block_rows = small_rows.shape[1]
    own_group = lax.axis_index("grp")
    own_id = small_ids[0, 0]
    own_count = small_count[0, 0]
    inner = jnp.arange(block_rows, dtype=jnp.int32)
    blocks = lax.all_gather(small_rows, "grp", axis=0, tiled=True)
    block_ids = lax.all_gather(small_ids[:, 0], "grp", axis=0, tiled=True)
    block_counts = lax.all_gather(small_count[:, 0], "grp", axis=0, tiled=True)

    def visit_block(offset, current):
        keys = lax.dynamic_index_in_dim(blocks, offset, 0, keepdims=False)
        key_id = lax.dynamic_index_in_dim(block_ids, offset, 0, keepdims=False)
        key_count = lax.dynamic_index_in_dim(block_counts, offset, 0, keepdims=False)
        source = offset

        def compute(previous):
            scores = jnp.einsum(
                "qd,kd->qk", small_rows[0], keys, preferred_element_type=jnp.float32
            )
            other = (source != own_group) | (inner[:, None] != inner[None, :])
            valid = (
                (inner[:, None] < own_count)
                & (inner[None, :] < key_count)
                & other
                & (key_id == own_id)
            )
            return jnp.maximum(previous, jnp.max(jnp.where(valid, scores, -2.0), axis=1))

        return compute(current)

    small_best = lax.fori_loop(
        0, blocks.shape[0], visit_block, jnp.full((block_rows,), -1.0, jnp.float32)
    )
    small_max = jnp.where(inner < own_count, small_best, 0.0).reshape(1, 1, block_rows)
    return (large_max, small_max)


def solution(mesh):
    placed = (
        P(("grp", "blk"), None),
        P("grp"),
        P("grp", "blk", None, None),
        P("grp", "blk"),
        P("grp", "blk"),
    )
    return jax.shard_map(
        body,
        mesh=mesh,
        in_specs=placed,
        out_specs=(P(("grp", "blk")), P("grp", "blk", None)),
        check_vma=False,
    )
```

profile of v0, /device:TPU:1, one launch (start us, length us, event | category | flops | bytes accessed | tf_op | source)
XLA Modules:
  0.0 302.0 jit_solution(6593927107855855079)
XLA Ops:
  7.2 1.4 fusion.17
  8.6 2.3 fusion.18
  11.2 1.0 fusion.20
  14.1 0.7 bitcast_dynamic-update-slice_fusion.1
  14.8 0.7 bitcast_dynamic-update-slice_fusion
  15.5 11.4 %all-reduce.2 = (s32[8]{0:T(128)S(1)}, s32[8]{0:T(128)S(1)}) all-reduce(s32[8]{0:T(128)S(1)} %bitcast_dynamic-update-slice_fusion.1, s32[8]{0:T(128)S(1)} %bitcast_dynamic-update-slice_fusion), channel_id=2, replica_groups=mesh['grp'=8,'blk'=32] {'grp'}, use_global_device_ids=true, to_apply=%add | all-reduce | flops 16 | bytes 128 | tf_op jit(solution)/shard_map/all_gather | solution.py:57
  27.6 80.8 %all-gather.8.cloned.1.call-done = bf16[8,1,512,768]{3,2,1,0:T(8,128)(2,1)} async-done(((bf16[1,1,512,768]{3,2,1,0:T(8,128)(2,1)}), bf16[8,1,512,768]{3,2,1,0:T(8,128)(2,1)}) %all-gather.8.cloned.1.call-update) | async-done | bytes 6291472 | tf_op jit(solution)/shard_map/all_gather | solution.py:55
  108.4 45.0 %while.30 = (s32[]{:T(128)}, f32[512]{0:T(512)S(1)}, s32[]{:T(128)}, s32[8]{0:T(128)S(1)}, s32[]{:T(128)}, /*index=5*/s32[8]{0:T(128)S(1)}, s32[]{:T(128)}, bf16...) while((s32[]{:T(128)}, f32[512]{0:T(512)S(1)}, ...), condition=%wide.region_7.8_spmd.clone.clone, body=%wide.region_5.7_spmd.clone.clone.sunk | while | flops 404489728 | bytes 1583287 | solution.py:80
  110.9 1.3 iota_compare_fusion.5
  112.2 1.8 fusion.35
  116.5 1.3 iota_compare_fusion.5
  117.8 1.8 fusion.35
  122.1 1.3 iota_compare_fusion.5
  123.4 1.8 fusion.35
  127.8 1.3 iota_compare_fusion.5
  129.0 1.9 fusion.35
  133.4 1.3 iota_compare_fusion.5
  134.7 1.8 fusion.35
  139.1 1.3 iota_compare_fusion.5
  140.3 1.8 fusion.35
  144.7 1.3 iota_compare_fusion.5
  146.0 1.8 fusion.35
  150.3 1.3 iota_compare_fusion.5
  151.6 1.8 fusion.35
  154.1 65.3 %all-gather.6.cloned.1.call-done = bf16[12288,768]{1,0:T(8,128)(2,1)} async-done(((bf16[384,768]{1,0:T(8,128)(2,1)}), bf16[12288,768]{1,0:T(8,128)(2,1)}) %all-gather.6.cloned.1.call-update) | async-done | bytes 18874384 | tf_op jit(solution)/shard_map/all_gather | solution.py:32
  219.4 75.2 %while.29 = (s32[]{:T(128)}, f32[384]{0:T(512)S(1)}, s32[]{:T(128)}, bf16[12288,768]{1,0:T(8,128)(2,1)}, bf16[384,768]{1,0:T(8,128)(2,1)S(1)}, /*index=5*/s32[]{:T(128)}, s32[]{:T(128)}, s32[]{:T(128)}, s32[]{:T(128)}, s32[]{:T(128)}) while((s32[]{:T(128)}, f32[384]{0:T(512)S(1)}, s32[]{:T(128)}, bf16[12288,768]{1,0:T(8,128)(2,1)}, ...), condition=%wide.region_3.4_spmd.clone, body=%wide.region_1.3_spmd.clone.sunk | while | flops 302976000 | bytes 1391553 | solution.py:47
  219.4 0.7 broadcast_compare_fusion.4
  220.0 0.7 broadcast_compare_fusion.5
  220.7 1.7 fusion.32
  222.5 0.7 broadcast_compare_fusion.4
  223.2 0.7 broadcast_compare_fusion.5
  223.8 1.7 fusion.32
  225.6 0.7 broadcast_compare_fusion.4
  226.3 0.7 broadcast_compare_fusion.5
  227.0 1.7 fusion.32
  228.8 0.7 broadcast_compare_fusion.4
  229.4 0.7 broadcast_compare_fusion.5
  230.1 1.8 fusion.32
  231.9 0.7 broadcast_compare_fusion.4
  232.6 0.7 broadcast_compare_fusion.5
  233.2 1.7 fusion.32
  235.1 0.7 broadcast_compare_fusion.4
  235.7 0.7 broadcast_compare_fusion.5
  236.4 1.7 fusion.32
  238.2 0.7 broadcast_compare_fusion.4
  238.8 0.7 broadcast_compare_fusion.5
  239.5 1.7 fusion.32
  242.6 1.7 fusion.32
  245.8 1.7 fusion.32
  248.9 1.7 fusion.32
  252.0 1.7 fusion.32
  255.2 1.7 fusion.32
  258.3 1.7 fusion.32
  261.4 1.7 fusion.32
  264.6 1.7 fusion.32
  267.7 1.7 fusion.32
  270.8 1.7 fusion.32
  274.0 1.7 fusion.32
  277.1 1.7 fusion.32
  280.2 1.7 fusion.32
  283.4 1.7 fusion.32
  286.5 1.7 fusion.32
  289.6 1.7 fusion.32
  292.8 1.7 fusion.32
  (152 shorter events, 34.4 us)
Async XLA Ops:
  7.2 3.8 %copy-start.1 = (bf16[384,768]{1,0:T(8,128)(2,1)S(1)}, bf16[384,768]{1,0:T(8,128)(2,1)}, u32[]{:S(2)}) copy-start(bf16[384,768]{1,0:T(8,128)(2,1)} %param.9) | copy-start | bytes 1769476
  7.2 101.3 %all-gather.8.cloned.1.call-start = ((), (), s32[]{:S(2)}) async-start(), calls=%async_computation.1 | async-start | bytes 7077888 | tf_op jit(solution)/shard_map/all_gather | solution.py:55
  10.9 2.6 copy-start.3
  10.9 97.5 %copy-start = (bf16[1,1,512,768]{3,2,1,0:T(8,128)(2,1)S(1)}, bf16[1,1,512,768]{3,2,1,0:T(8,128)(2,1)}, u32[]{:S(2)}) copy-start(bf16[1,1,512,768]{3,2,1,0:T(8,128)(2,1)} %fusion.18) | copy-start | bytes 2359300
  10.9 208.4 %all-gather.6.cloned.1.call-start = ((), (), s32[]{:S(2)}) async-start(), calls=%async_computation | async-start | bytes 19464192 | tf_op jit(solution)/shard_map/all_gather | solution.py:32
  108.4 110.9 %copy-start.2 = (bf16[384,768]{1,0:T(8,128)(2,1)S(1)}, bf16[384,768]{1,0:T(8,128)(2,1)}, u32[]{:S(2)}) copy-start(bf16[384,768]{1,0:T(8,128)(2,1)} %fusion.20) | copy-start | bytes 1769476
Sparse Core Ops, SparseCore 0:
  11.1 97.3 all-gather.7
  110.3 109.0 all-gather.5
where the time goes:
time: 304 us; the launch traced here: 302 us
  waiting for transfers between devices  146 us (48%)
  matrix products  56.6 us (19%)
  other arithmetic  48.2 us (16%)
  between operations  16.1 us (5%)
  loops' own time  11.9 us (4%)
  local copies, waits for them, and re-layouts  11.5 us (4%)
  blocking collectives  11.4 us (4%)
    all_gather x1, waiting for transfers between devices, body(): blocks = lax.all_gather(small_rows, 'grp', axis=0, tiled=True)  80.8 us
    all_gather x1, waiting for transfers between devices, body(): piece = lax.all_gather(local_rows, 'blk', axis=0, tiled=True)  65.3 us
    dot_general x24, matrix products, masked_scores(): jnp.einsum('qd,kd->qk', queries, keys, preferred_element_type=jnp.float32)  42 us
    lt x24, other arithmetic, masked_scores(): query_pos[:, None] < live_count  15.7 us
    lt x24, other arithmetic, masked_scores(): key_pos[None, :] < live_count  15.7 us
    dot_general x8, matrix products, compute(): jnp.einsum('qd,kd->qk', small_rows[0], keys, preferred_element_type=jnp.f...  14.7 us
    all_gather x1, blocking collectives, body(): block_counts = lax.all_gather(small_count[:, 0], 'grp', axis=0, tiled=True)  11.4 us
    another operation x1, loops' own time, body(): lax.fori_loop(0, blocks.shape[0], visit_block, jnp.full((block_rows,), -1...  10.5 us
  transfers between devices with their start and end apart: 2, of which 2 were waited for; matrix products, arithmetic and copies ran while one was open for 13% of the time, Pallas kernels for 0%

commit v1 on v0

v1 whole, which is shorter than its diff:
```python
import jax
import jax.numpy as jnp
from jax import lax
from jax.experimental import pallas as pl
from jax.experimental.pallas import tpu as pltpu
from jax.sharding import PartitionSpec as P

EPSILON = 1e-06
MESH = pl.DeviceIdType.MESH
DEAD = -4.0

N_X, N_Y, N_Z = 4, 4, 8
ROWS, D, BR = 384, 768, 512
SUB = 128
PIECES = ((0, 128), (128, 128), (256, 64), (320, 64))
N_PIECE = len(PIECES)
HALF = BR // 2


def unit_rows(embedding):
    widened = embedding.astype(jnp.float32)
    inverse = lax.rsqrt(jnp.sum(widened * widened, axis=-1, keepdims=True) + EPSILON)
    return (widened * inverse).astype(jnp.bfloat16)


def scores_of(rows, cols):
    return lax.dot_general(
        rows, cols, (((1,), (1,)), ((), ())), preferred_element_type=jnp.float32
    )


def over_rows(s):
    m, n = s.shape
    return jnp.max(s.reshape(m // 8, 8, n), axis=0)


def over_cols(s):
    best = s[:, :128]
    for first in range(128, s.shape[1], 128):
        best = jnp.maximum(best, s[:, first : first + 128])
    return best


def turned(best):
    return jnp.concatenate(
        [over_rows(best[f : f + 128].T) for f in range(0, best.shape[0], 128)], axis=1
    )


def add_rows_bias(s, bias):
    return jnp.concatenate(
        [s[:, f : f + 128] + bias for f in range(0, s.shape[1], 128)], axis=1
    )


def kernel(
    large_count, small_id, small_count, large_emb, small_emb,
    large_out, small_out,
    win, far, near, across, meta, meta_across,
    best_win, best_far_rows, best_far, best_near, best_near_rows, best_across,
    got_large, got_small,
    own_s, own_r, fwd_s, fwd_r, sib_s, sib_r, cross_s, cross_r, diag_s, diag_r,
    near_s, near_r, hop_s, hop_r, across_s, across_r, meta_s, meta_r,
    lres_s, lres_r, sres_s, sres_r,
):
    grp, blk = lax.axis_index("grp"), lax.axis_index("blk")
    y, xh = grp // 2, lax.rem(grp, 2)
    c = lax.rem(blk, 2)
    z = lax.rem(blk // 2, N_Z)
    xl = blk // (2 * N_Z)

    def on_z(dz, flip_x=0, flip_c=0):
        z2 = lax.rem(z + dz + N_Z, N_Z)
        x2 = lax.rem(xl + flip_x, 2)
        c2 = lax.rem(c + flip_c, 2)
        return (grp, (x2 * N_Z + z2) * 2 + c2)

    def on_y(dy, flip_x=0):
        return (lax.rem(y + dy + N_Y, N_Y) * 2 + lax.rem(xh + flip_x, 2), blk)

    def remote(src, dst, send, recv, device):
        return pltpu.make_async_remote_copy(
            src_ref=src, dst_ref=dst, send_sem=send, recv_sem=recv,
            device_id=device, device_id_type=MESH,
        )

    wide = xh == c
    thin = xh != c

    partners = [on_z(d) for d in (-2, -1, 1, 2)] + [on_y(d) for d in (-1, 1, 2)]
    partners += [on_y(0, 1), on_z(0, 1, 0), on_z(0, 0, 1)]
    partners += [on_z(d, fx, fc) for d in (-2, 2) for fx, fc in ((0, 1), (1, 0), (1, 1))]
    barrier = pltpu.get_barrier_semaphore()
    for partner in partners:
        pl.semaphore_signal(barrier, inc=1, device_id=partner, device_id_type=MESH)

    def own_copy(i, k):
        rows = pl.ds(PIECES[k][0], PIECES[k][1])
        return remote(win.at[2, rows], win.at[1 + 2 * i, rows], own_s.at[i, k], own_r.at[i, k], on_z(1 - 2 * i))

    def fwd_copy(i, k):
        rows = pl.ds(PIECES[k][0], PIECES[k][1])
        return remote(win.at[1 + 2 * i, rows], win.at[4 * i, rows], fwd_s.at[i, k], fwd_r.at[i, k], on_z(1 - 2 * i))

    def far_rows(kind, k):
        first, n = PIECES[k]
        return far.at[first // SUB, pl.ds(kind * SUB + first % SUB, n)]

    def sib_copy(k):
        rows = pl.ds(PIECES[k][0], PIECES[k][1])
        return remote(win.at[4, rows], far_rows(0, k), sib_s.at[k], sib_r.at[k], on_z(0, 0, 1))

    def cross_copy(k):
        rows = pl.ds(PIECES[k][0], PIECES[k][1])
        return remote(win.at[4, rows], far_rows(1, k), cross_s.at[k], cross_r.at[k], on_z(0, 1, 0))

    def diag_copy(k):
        return remote(far_rows(1, k), far_rows(2, k), diag_s.at[k], diag_r.at[k], on_z(0, 0, 1))

    def near_copy(i, h):
        rows = pl.ds(((1 - i) ^ h) * HALF, HALF)
        return remote(near.at[1, rows], near.at[2 * i, rows], near_s.at[i, h], near_r.at[i, h], on_y(1 - 2 * i))

    def hop_copy(i):
        rows = pl.ds((1 - i) * HALF, HALF)
        return remote(near.at[2 * i, rows], near.at[3, rows], hop_s.at[i], hop_r.at[i], on_y(1 - 2 * i))

    def across_copy():
        return remote(near.at[1], across, across_s.at[0], across_r.at[0], on_y(0, 1))

    def meta_copy(n):
        dst = meta_across if n == 3 else meta.at[(0, 2, 3)[n]]
        return remote(meta.at[1], dst, meta_s.at[n], meta_r.at[n], on_y(0, 1) if n == 3 else on_y((1, -1, 2)[n]))

    def large_result(n):
        src = best_win.at[(0, 1, 3, 4)[n]] if n < 4 else best_far.at[n - 4]
        to = on_z((-2, -1, 1, 2)[n]) if n < 4 else on_z(2, *((0, 1), (1, 0), (1, 1))[n - 4])
        return remote(src, got_large.at[n], lres_s.at[n], lres_r.at[n], to)

    def small_result(n):
        src = best_across if n == 3 else best_near.at[(0, 2, 3)[n]]
        slot = min(n, 2)
        to = on_y(0, 1) if n == 3 else on_y((-1, 1, 2)[n])
        return remote(src, got_small.at[slot], sres_s.at[n], sres_r.at[slot], to)

    for k, (first, n) in enumerate(PIECES):
        win[2, first : first + n] = unit_rows(large_emb[first : first + n])
        if k == 0:
            meta[1] = jnp.full((8, 128), small_id[0, 0] * 1024 + small_count[0, 0], jnp.int32)
            pl.semaphore_wait(barrier, len(partners))
        for i in range(2):
            own_copy(i, k).start()
    for n in range(4):
        meta_copy(n).start()
    for h in (1, 0):
        near[1, h * HALF : (h + 1) * HALF] = unit_rows(small_emb[h * HALF : (h + 1) * HALF])
        near_copy(1 - h, 0).start()
    for i in range(2):
        near_copy(i, 1).start()

    @pl.when(thin)
    def _():
        across_copy().start()

    best_win[...] = jnp.full(best_win.shape, -1.0, jnp.float32)
    best_far_rows[...] = jnp.full(best_far_rows.shape, -1.0, jnp.float32)
    best_near[...] = jnp.full(best_near.shape, -1.0, jnp.float32)
    best_near_rows[...] = jnp.full(best_near_rows.shape, -1.0, jnp.float32)

    count = large_count[0]

    def first_position(dz, flip_x=0, flip_c=0):
        return on_z(dz, flip_x, flip_c)[1] * ROWS

    def col_bias(slot):
        z2 = lax.rem(z + slot - 2 + N_Z, N_Z)
        first = ((xl * N_Z + z2) * 2 + c) * ROWS
        at = first + lax.broadcasted_iota(jnp.int32, (1, ROWS), 1)
        return jnp.where(at < count, 0.0, DEAD)

    def row_bias(first, n):
        at = first + lax.broadcasted_iota(jnp.int32, (n, 128), 0)
        return jnp.where(at < count, 0.0, DEAD)

    def far_bias(k):
        return jnp.concatenate(
            [row_bias(first_position(2, fx, fc) + k * SUB, SUB) for fx, fc in ((0, 1), (1, 0), (1, 1))], axis=0
        )

    def pair(rows, bias, slot):
        s = scores_of(rows, win[slot])
        best_win[slot] = jnp.maximum(best_win[slot], over_rows(add_rows_bias(s, bias)))
        return over_cols(s + col_bias(slot))

    def win_pairs(slot, lowest, n):
        for f in range(0, ROWS, SUB):
            rows = win[slot, f : f + SUB]
            bias = row_bias(first_position(slot - 2) + f, SUB)

            def step(j, best):
                return jnp.maximum(best, pair(rows, bias, lowest + j))

            best = lax.fori_loop(0, n, step, jnp.full((SUB, 128), -1.0, jnp.float32))
            best_win[slot, :, f : f + SUB] = jnp.maximum(best_win[slot, :, f : f + SUB], turned(best))

    def far_pairs(k, lowest, n):
        bias = far_bias(k)

        def step(j, carry):
            best = pair(far[k], bias, lowest + j)
            best_far_rows[k] = jnp.maximum(best_far_rows[k], best)
            return carry

        lax.fori_loop(0, n, step, 0)

    def far_ends(k):
        bias = far_bias(k)
        for f, n, slot in ((0, SUB, 4 - 4 * c), (SUB, 2 * SUB, 4 - 4 * xl)):
            best = pair(far[k, f : f + n], bias[f : f + n], slot)
            best_far_rows[k, f : f + n] = jnp.maximum(best_far_rows[k, f : f + n], best)

    def far_done(k):
        best = turned(best_far_rows[k])
        for kind in range(3):
            best_far[kind, :, k * SUB : (k + 1) * SUB] = best[:, kind * SUB : (kind + 1) * SUB]

    def large_self():
        s = scores_of(win[2], win[2])
        r = lax.broadcasted_iota(jnp.int32, s.shape, 0)
        q = lax.broadcasted_iota(jnp.int32, s.shape, 1)
        s = add_rows_bias(jnp.where(r == q, DEAD, s), row_bias(first_position(0), ROWS))
        best_win[2] = jnp.maximum(best_win[2], over_rows(s))

    def small_col_bias(meta_row, meta_col, first, n):
        at = first + lax.broadcasted_iota(jnp.int32, (1, n), 1)
        r = jnp.concatenate([meta_row[0:1]] * (n // 128), axis=1)
        q = jnp.concatenate([meta_col[0:1]] * (n // 128), axis=1)
        return jnp.where(((r >> 10) == (q >> 10)) & (at < (q & 1023)), 0.0, DEAD)

    def small_row_bias(meta_row, meta_col, first, n):
        at = first + lax.broadcasted_iota(jnp.int32, (n, 128), 0)
        r, q = meta_row[0:1], meta_col[0:1]
        live = jnp.where((r >> 10) == (q >> 10), r & 1023, 0)
        return jnp.where(at < live, 0.0, DEAD)

    def small_self():
        for f in range(0, BR, HALF):
            s = scores_of(near[1, f : f + HALF], near[1])
            r = f + lax.broadcasted_iota(jnp.int32, s.shape, 0)
            q = lax.broadcasted_iota(jnp.int32, s.shape, 1)
            bias = small_row_bias(meta[1], meta[1], f, HALF)
            s = add_rows_bias(jnp.where(r == q, DEAD, s), bias)
            best_near[1] = jnp.maximum(best_near[1], over_rows(s))

    def one_above():
        def step(h, carry):
            f = pl.multiple_of(h * HALF, HALF)
            s = scores_of(near[2, pl.ds(f, HALF)], near[1])
            rb = small_row_bias(meta[2], meta[1], f, HALF)
            cb = small_col_bias(meta[2], meta[1], 0, BR)
            best_near[1] = jnp.maximum(best_near[1], over_rows(add_rows_bias(s, rb)))
            best_near_rows[0, pl.ds(f, HALF)] = jnp.maximum(best_near_rows[0, pl.ds(f, HALF)], over_cols(s + cb))
            return carry

        lax.fori_loop(0, 2, step, 0)

    def two_apart():
        low = 1 - y // 2

        def step(h, carry):
            fr = pl.multiple_of((h * low + (1 - low)) * HALF, HALF)
            fc = pl.multiple_of(h * (1 - low) * HALF, HALF)
            s = scores_of(near[2, pl.ds(fr, HALF)], near[0, pl.ds(fc, HALF)])
            rb = small_row_bias(meta[2], meta[0], fr, HALF)
            cb = small_col_bias(meta[2], meta[0], fc, HALF)
            best_near[0, :, pl.ds(fc, HALF)] = jnp.maximum(
                best_near[0, :, pl.ds(fc, HALF)], over_rows(add_rows_bias(s, rb))
            )
            best_near_rows[0, pl.ds(fr, HALF)] = jnp.maximum(best_near_rows[0, pl.ds(fr, HALF)], over_cols(s + cb))
            return carry

        lax.fori_loop(0, 2, step, 0)

    def with_across(lowest, n):
        def step(j, carry):
            slot = lowest + j // 2
            f = pl.multiple_of(lax.rem(j, 2) * HALF, HALF)
            s = scores_of(across[pl.ds(f, HALF)], near[slot])
            rb = small_row_bias(meta_across[...], meta[slot], f, HALF)
            cb = small_col_bias(meta_across[...], meta[slot], 0, BR)
            best_near[slot] = jnp.maximum(best_near[slot], over_rows(add_rows_bias(s, rb)))
            best_near_rows[1, pl.ds(f, HALF)] = jnp.maximum(best_near_rows[1, pl.ds(f, HALF)], over_cols(s + cb))
            return carry

        lax.fori_loop(0, 2 * n, step, 0)

    large_self()
    for n in range(4):
        meta_copy(n).wait_recv()
    small_self()
    for k in range(N_PIECE):
        for i in range(2):
            own_copy(i, k).wait_recv()
            fwd_copy(i, k).start()
        if k == 1:
            for i in range(2):
                near_copy(i, 0).wait_recv()

            @pl.when(wide)
            def _():
                for i in range(2):
                    hop_copy(i).start()
                across_copy().wait_recv()
                with_across(1, 1)

    win_pairs(3, 1, 2)

    def take(k):
        fwd_copy(1, k).wait_recv()
        sib_copy(k).start()
        cross_copy(k).start()

    def pass_on(k):
        cross_copy(k).wait_recv()
        diag_copy(k).start()

    take(0)
    for i in range(2):
        near_copy(i, 1).wait_recv()
    one_above()
    two_apart()

    @pl.when(wide)
    def _():
        with_across(0, 1)
        with_across(2, 1)

    take(1)
    pass_on(0)

    @pl.when(wide)
    def _():
        for i in range(2):
            hop_copy(i).wait_recv()
        with_across(3, 1)
        best_across[...] = turned(best_near_rows[1])
    best_near[2] = jnp.maximum(best_near[2], turned(best_near_rows[0]))
    for n in range(2):
        small_result(n).start()

    @pl.when(wide)
    def _():
        for n in (2, 3):
            small_result(n).start()

    sib_copy(0).wait_recv()
    diag_copy(0).wait_recv()
    far_pairs(0, 1, 3)
    take(2)
    pass_on(1)
    sib_copy(1).wait_recv()
    diag_copy(1).wait_recv()
    far_pairs(1, 1, 3)
    take(3)
    pass_on(2)
    for k in range(N_PIECE):
        fwd_copy(0, k).wait_recv()
    win_pairs(4, 0, 2)
    for k in range(2):
        far_ends(k)
        far_done(k)
    pass_on(3)
    for k in (2, 3):
        sib_copy(k).wait_recv()
        diag_copy(k).wait_recv()
    far_pairs(2, 1, 3)
    far_ends(2)
    far_done(2)

    for n in range(7):
        large_result(n).start()
    at = lax.broadcasted_iota(jnp.int32, (1, BR), 1)
    for n in range(3):
        small_result(n).wait_recv()
    best = best_near[1]
    for n in range(3):
        best = jnp.maximum(best, got_small[n])
    small_out[...] = jnp.where(at < small_count[0, 0], jnp.max(best, axis=0, keepdims=True), 0.0)
    at = first_position(0) + lax.broadcasted_iota(jnp.int32, (1, ROWS), 1)
    for n in range(7):
        large_result(n).wait_recv()
    best = best_win[2]
    for n in range(7):
        best = jnp.maximum(best, got_large[n])
    large_out[...] = jnp.where(at < count, jnp.max(best, axis=0, keepdims=True), 0.0)

    for k in range(N_PIECE):
        for i in range(2):
            own_copy(i, k).wait_send()
            fwd_copy(i, k).wait_send()
        sib_copy(k).wait_send()
        cross_copy(k).wait_send()
        diag_copy(k).wait_send()
    for i in range(2):
        for h in range(2):
            near_copy(i, h).wait_send()
    for n in range(4):
        meta_copy(n).wait_send()
    for n in range(7):
        large_result(n).wait_send()
    for n in range(2):
        small_result(n).wait_send()

    @pl.when(wide)
    def _():
        for i in range(2):
            hop_copy(i).wait_send()
        for n in (2, 3):
            small_result(n).wait_send()

    @pl.when(thin)
    def _():
        across_copy().wait_send()


def body(large_emb, large_count, small_emb, small_ids, small_count):
    vmem = pl.BlockSpec(memory_space=pltpu.VMEM)
    smem = pl.BlockSpec(memory_space=pltpu.SMEM)
    dma = pltpu.SemaphoreType.DMA
    f32, bf16, i32 = jnp.float32, jnp.bfloat16, jnp.int32
    large, small = pl.pallas_call(
        kernel,
        out_shape=(jax.ShapeDtypeStruct((1, ROWS), f32), jax.ShapeDtypeStruct((1, BR), f32)),
        in_specs=[smem, smem, smem, vmem, vmem],
        out_specs=(vmem, vmem),
        scratch_shapes=[
            pltpu.VMEM((5, ROWS, D), bf16),
            pltpu.VMEM((ROWS // SUB, 3 * SUB, D), bf16),
            pltpu.VMEM((4, BR, D), bf16),
            pltpu.VMEM((BR, D), bf16),
            pltpu.VMEM((4, 8, 128), i32),
            pltpu.VMEM((8, 128), i32),
            pltpu.VMEM((5, 8, ROWS), f32),
            pltpu.VMEM((ROWS // SUB, 3 * SUB, 128), f32),
            pltpu.VMEM((3, 8, ROWS), f32),
            pltpu.VMEM((4, 8, BR), f32),
            pltpu.VMEM((2, BR, 128), f32),
            pltpu.VMEM((8, BR), f32),
            pltpu.VMEM((7, 8, ROWS), f32),
            pltpu.VMEM((3, 8, BR), f32),
            dma((2, N_PIECE)), dma((2, N_PIECE)), dma((2, N_PIECE)), dma((2, N_PIECE)),
            dma((N_PIECE,)), dma((N_PIECE,)), dma((N_PIECE,)), dma((N_PIECE,)), dma((N_PIECE,)), dma((N_PIECE,)),
            dma((2, 2)), dma((2, 2)), dma((2,)), dma((2,)), dma((1,)), dma((1,)), dma((4,)), dma((4,)),
            dma((7,)), dma((7,)), dma((4,)), dma((3,)),
        ],
        compiler_params=pltpu.CompilerParams(
            collective_id=0, has_side_effects=True, vmem_limit_bytes=48 * 2**20
        ),
        name="cluster_maxima",
    )(large_count, small_ids, small_count, large_emb, small_emb.reshape(BR, D))
    return large.reshape(ROWS), small.reshape(1, 1, BR)


def solution(mesh):
    placed = (
        P(("grp", "blk"), None),
        P("grp"),
        P("grp", "blk", None, None),
        P("grp", "blk"),
        P("grp", "blk"),
    )
    return jax.shard_map(
        body,
        mesh=mesh,
        in_specs=placed,
        out_specs=(P(("grp", "blk")), P("grp", "blk", None)),
        check_vma=False,
    )
```

time: 304 us -> 59.4 us (0.20)
  waiting for transfers between devices: 146 us -> 0 us
  matrix products: 56.6 us -> 0 us
  Pallas kernels: 0 us -> 53.3 us
  other arithmetic: 48.2 us -> 0.6 us
  between operations: 16.1 us -> 2.58 us
  loops' own time: 11.9 us -> 0 us
  blocking collectives: 11.4 us -> 0 us
  local copies, waits for them, and re-layouts: 11.5 us -> 2.77 us
    all_gather x2 -> x0, waiting for transfers between devices: 146 us -> none  [the longest x1 80.8 us: body(): blocks = lax.all_gather(small_rows, 'grp', axis=0, tiled=True)]
    dot_general x32 -> x0, matrix products: 56.6 us -> none  [the longest x24 42 us: masked_scores(): jnp.einsum('qd,kd->qk', queries, keys, preferred_element_type=jnp.float32)]
    pallas_call x0 -> x1, Pallas kernels: none -> 53.3 us  [body(): pl.pallas_call(kernel, out_shape=(jax.ShapeDtypeStruct((1, ROWS), f32), j...]
    lt x56 -> x0, other arithmetic: 41.5 us -> none  [the longest x24 15.7 us: masked_scores(): query_pos[:, None] < live_count]
    another operation x2 -> x0, loops' own time: 11.9 us -> none  [the longest x1 10.5 us: body(): lax.fori_loop(0, blocks.shape[0], visit_block, jnp.full((block_rows,), -1...]
    all_gather x1 -> x0, blocking collectives: 11.4 us -> none  [body(): block_counts = lax.all_gather(small_count[:, 0], 'grp', axis=0, tiled=True)]
    dynamic_slice x16 -> x0, local copies, waits for them, and re-layouts: 9.55 us -> none  [the longest x8 4.77 us: visit_block(): lax.dynamic_index_in_dim(block_counts, offset, 0, keepdims=False)]
    convert_element_type x2 -> x0, other arithmetic: 3.27 us -> none  [unit_rows(): return (widened * inverse).astype(jnp.bfloat16)]
  transfers between devices with their start and end apart: 2 -> 0, of which waited for: 2 -> 0; matrix products, arithmetic and copies ran while one was open for 13% -> 0% of each run, Pallas kernels for 0% -> 0%
where the time goes in v1:
time: 59.4 us; the launch traced here: 59.2 us
  Pallas kernels  53.3 us (90%)
  local copies, waits for them, and re-layouts  2.77 us (5%)
  between operations  2.58 us (4%)
  other arithmetic  0.6 us (1%)
    pallas_call x1, Pallas kernels, body(): pl.pallas_call(kernel, out_shape=(jax.ShapeDtypeStruct((1, ROWS), f32), j...  53.3 us
    unnamed x5, local copies, waits for them, and re-layouts  2.77 us

profile of v1, /device:TPU:1, one launch (start us, length us, event | category | flops | bytes accessed | tf_op | source)
XLA Modules:
  0.0 59.2 jit_solution(6334715451264164391)
XLA Ops:
  2.6 0.0 copy-start
  2.6 1.1 %copy-done = bf16[1,1,512,768]{3,2,1,0:T(8,128)(2,1)S(1)} copy-done((bf16[1,1,512,768]{3,2,1,0:T(8,128)(2,1)S(1)}, bf16[1,1,512,768]{3,2,1,0:T(8,128)(2,1)}, u32[]{:S(2)}) %copy-start) | copy-done | bytes 786456
  3.7 0.0 copy-start.1
  3.7 1.1 %copy-done.1 = bf16[384,768]{1,0:T(8,128)(2,1)S(1)} copy-done((bf16[384,768]{1,0:T(8,128)(2,1)S(1)}, bf16[384,768]{1,0:T(8,128)(2,1)}, u32[]{:S(2)}) %copy-start.1) | copy-done | bytes 589848
  4.8 53.3 %cluster_maxima.1 = (f32[1,384]{1,0:T(1,128)S(1)}, f32[1,512]{1,0:T(1,128)S(1)}) custom-call(s32[1]{0:T(128)S(6)} %copy.8.large_count, s32[1,1]{1,0:T(1,128)S(6)} %copy.9.small_id, s32[1,1]{1,0:T(1,128)S(6)} %copy.10.small_count, bf16[384,768]{1,0:T(8,128)(2,1)S(1)} %copy-done.1, bf16[512,768]{1,0:T(8,128)(2,1)S(1)} %bitcast.2), custom_call_target="tpu_custom_call" | custom-call | tf_op jit(solution)/shard_map/cluster_maxima/pallas_call | solution.py:431
  58.1 0.6 %reduce = f32[384]{0:T(512)} reduce(f32[1,384]{1,0:T(1,128)S(1)} %get-tuple-element.4, f32[]{:T(128)} %constant.5), dimensions={0}, to_apply=%get-tuple-element.4.reduce_sub_computation | reduce | bytes 3076 | tf_op jit(solution)/shard_map/cluster_maxima/pallas_call | solution.py:431
  58.7 0.6 copy.11
Async XLA Ops:
  2.6 1.1 %copy-start = (bf16[1,1,512,768]{3,2,1,0:T(8,128)(2,1)S(1)}, bf16[1,1,512,768]{3,2,1,0:T(8,128)(2,1)}, u32[]{:S(2)}) copy-start(bf16[1,1,512,768]{3,2,1,0:T(8,128)(2,1)} %param.7) | copy-start | bytes 2359300
  3.7 1.1 %copy-start.1 = (bf16[384,768]{1,0:T(8,128)(2,1)S(1)}, bf16[384,768]{1,0:T(8,128)(2,1)}, u32[]{:S(2)}) copy-start(bf16[384,768]{1,0:T(8,128)(2,1)} %large_emb.1) | copy-start | bytes 1769476

commit v2 on v1

v2 whole, which is shorter than its diff:
```python
import jax
import jax.numpy as jnp
from jax import lax
from jax.experimental import pallas as pl
from jax.experimental.pallas import tpu as pltpu
from jax.sharding import PartitionSpec as P

EPSILON = 1e-06
MESH = pl.DeviceIdType.MESH
DEAD = -4.0

N_X, N_Y, N_Z = 4, 4, 8
ROWS, D, BR = 384, 768, 512
SUB = 128
PIECES = ((0, 128), (128, 128), (256, 128))
N_PIECE = len(PIECES)
HALF = BR // 2
PLACE = {1: 0, 0: 1, -1: 2, -2: 3, 2: 4}
KINDS = ((0, 1), (1, 0), (1, 1))


def unit_rows(embedding):
    widened = embedding.astype(jnp.float32)
    inverse = lax.rsqrt(jnp.sum(widened * widened, axis=-1, keepdims=True) + EPSILON)
    return (widened * inverse).astype(jnp.bfloat16)


def scores_of(rows, cols):
    return lax.dot_general(
        rows, cols, (((1,), (1,)), ((), ())), preferred_element_type=jnp.float32
    )


def over_rows(s):
    m, n = s.shape
    return jnp.max(s.reshape(m // 8, 8, n), axis=0)


def over_cols(s):
    best = s[:, :128]
    for first in range(128, s.shape[1], 128):
        best = jnp.maximum(best, s[:, first : first + 128])
    return best


def turned(best):
    return jnp.concatenate(
        [over_rows(best[f : f + 128].T) for f in range(0, best.shape[0], 128)], axis=1
    )


def add_rows_bias(s, bias):
    return jnp.concatenate(
        [s[:, f : f + 128] + bias for f in range(0, s.shape[1], 128)], axis=1
    )


def kernel(
    large_count_in, small_id_in, small_count_in, large_emb, small_emb,
    large_out, small_out,
    raw_large, raw_small,
    win, far, near, across, meta, meta_across, live_cols,
    best_win, best_far_rows, best_far, best_near, best_near_rows, best_across,
    got_large, got_small,
    large_count, small_id, small_count,
    scalar_r, raw_r, own_s, own_r, fwd_s, fwd_r, sib_s, sib_r, cross_s, cross_r, diag_s, diag_r,
    near_s, near_r, hop_s, hop_r, across_s, across_r, meta_s, meta_r,
    lres_s, lres_r, sres_s, sres_r,
):
    grp, blk = lax.axis_index("grp"), lax.axis_index("blk")
    y, xh = grp // 2, lax.rem(grp, 2)
    c = lax.rem(blk, 2)
    z = lax.rem(blk // 2, N_Z)
    xl = blk // (2 * N_Z)

    def on_z(dz, flip_x=0, flip_c=0):
        z2 = lax.rem(z + dz + N_Z, N_Z)
        x2 = lax.rem(xl + flip_x, 2)
        c2 = lax.rem(c + flip_c, 2)
        return (grp, (x2 * N_Z + z2) * 2 + c2)

    def on_y(dy, flip_x=0):
        return (lax.rem(y + dy + N_Y, N_Y) * 2 + lax.rem(xh + flip_x, 2), blk)

    def remote(src, dst, send, recv, device):
        return pltpu.make_async_remote_copy(
            src_ref=src, dst_ref=dst, send_sem=send, recv_sem=recv,
            device_id=device, device_id_type=MESH,
        )

    wide = xh == c
    thin = xh != c

    def raw_copy(n):
        if n < 2:
            rows = pl.ds((0, PIECES[0][1])[n], (PIECES[0][1], ROWS - PIECES[0][1])[n])
            return pltpu.make_async_copy(large_emb.at[rows], raw_large.at[rows], raw_r.at[n])
        return pltpu.make_async_copy(small_emb, raw_small, raw_r.at[n])

    def win_rows(dz, k):
        first, n = PIECES[k]
        return win.at[pl.ds(PLACE[dz] * ROWS + first, n)]

    def own_copy(i, k):
        src = win_rows(0, k) if k else large_emb.at[pl.ds(*PIECES[0])]
        return remote(src, win_rows(2 * i - 1, k), own_s.at[i, k], own_r.at[i, k], on_z(1 - 2 * i))

    def fwd_copy(i, k):
        return remote(win_rows(2 * i - 1, k), win_rows(4 * i - 2, k), fwd_s.at[i, k], fwd_r.at[i, k], on_z(1 - 2 * i))

    def far_rows(kind, k):
        first, n = PIECES[k]
        return far.at[first // SUB, pl.ds(kind * SUB + first % SUB, n)]

    def sib_copy(k):
        return remote(win_rows(2, k), far_rows(0, k), sib_s.at[k], sib_r.at[k], on_z(0, 0, 1))

    def cross_copy(k):
        return remote(win_rows(2, k), far_rows(1, k), cross_s.at[k], cross_r.at[k], on_z(0, 1, 0))

    def diag_copy(k):
        return remote(far_rows(1, k), far_rows(2, k), diag_s.at[k], diag_r.at[k], on_z(0, 0, 1))

    def near_copy(i, h):
        rows = pl.ds(((1 - i) ^ h) * HALF, HALF)
        return remote(near.at[1, rows], near.at[2 * i, rows], near_s.at[i, h], near_r.at[i, h], on_y(1 - 2 * i))

    def hop_copy(i):
        rows = pl.ds((1 - i) * HALF, HALF)
        return remote(near.at[2 * i, rows], near.at[3, rows], hop_s.at[i], hop_r.at[i], on_y(1 - 2 * i))

    def across_copy():
        return remote(near.at[1], across, across_s.at[0], across_r.at[0], on_y(0, 1))

    def meta_copy(n):
        if n == 0:
            return remote(meta.at[1], meta.at[0], meta_s.at[0], meta_r.at[0], on_y(1))
        if n == 1:
            return remote(meta.at[1], meta.at[2], meta_s.at[1], meta_r.at[1], on_y(-1))
        if n == 2:
            return remote(meta.at[1], meta_across, meta_s.at[2], meta_r.at[2], on_y(0, 1))
        return remote(meta.at[0], meta.at[3], meta_s.at[3], meta_r.at[3], on_y(1))

    def large_result(n):
        src = best_far.at[n - 4] if n > 3 else best_win.at[:, pl.ds(PLACE[(-2, -1, 1, 2)[n]] * ROWS, ROWS)]
        to = on_z((-2, -1, 1, 2)[n]) if n < 4 else on_z(2, *KINDS[n - 4])
        return remote(src, got_large.at[n], lres_s.at[n], lres_r.at[n], to)

    def small_result(n):
        src = best_across if n == 3 else best_near.at[(0, 2, 3)[n]]
        slot = min(n, 2)
        to = on_y(0, 1) if n == 3 else on_y((-1, 1, 2)[n])
        return remote(src, got_small.at[slot], sres_s.at[n], sres_r.at[slot], to)

    def scalar_copy(n):
        src, dst = ((large_count_in, large_count), (small_id_in, small_id), (small_count_in, small_count))[n]
        return pltpu.make_async_copy(src, dst, scalar_r.at[n])

    partners = [on_z(-1), on_z(1), on_y(-1), on_y(1), on_y(0, 1), on_z(0, 1, 0), on_z(0, 0, 1)]
    barrier = pltpu.get_barrier_semaphore()
    for partner in partners:
        pl.semaphore_signal(barrier, inc=1, device_id=partner, device_id_type=MESH)
    for n in range(3):
        raw_copy(n).start()
    for n in range(3):
        scalar_copy(n).start()
    pl.semaphore_wait(barrier, len(partners))
    for i in range(2):
        own_copy(i, 0).start()
    own_first = PLACE[0] * ROWS
    for k, (first, n) in enumerate(PIECES):
        if k < 2:
            raw_copy(k).wait()
        win[own_first + first : own_first + first + n] = unit_rows(raw_large[first : first + n])
        if k:
            for i in range(2):
                own_copy(i, k).start()
    for n in range(3):
        scalar_copy(n).wait()
    meta[1] = jnp.full((8, 128), small_id[0, 0] * 1024 + small_count[0, 0], jnp.int32)
    for n in range(3):
        meta_copy(n).start()
    raw_copy(2).wait()
    for h in (1, 0):
        near[1, h * HALF : (h + 1) * HALF] = unit_rows(raw_small[h * HALF : (h + 1) * HALF])
        near_copy(1 - h, 0).start()
    for i in range(2):
        near_copy(i, 1).start()

    @pl.when(thin)
    def _():
        across_copy().start()

    best_win[...] = jnp.full(best_win.shape, -1.0, jnp.float32)
    best_near[...] = jnp.full(best_near.shape, -1.0, jnp.float32)
    best_near_rows[...] = jnp.full(best_near_rows.shape, -1.0, jnp.float32)

    count = large_count[0]

    def first_position(dz, flip_x=0, flip_c=0):
        return on_z(dz, flip_x, flip_c)[1] * ROWS

    for dz, place in PLACE.items():
        at = first_position(dz) + lax.broadcasted_iota(jnp.int32, (1, ROWS), 1)
        live_cols[:, place * ROWS : (place + 1) * ROWS] = jnp.where(at < count, 0.0, DEAD)

    def row_bias(first, n):
        at = first + lax.broadcasted_iota(jnp.int32, (n, 128), 0)
        return jnp.where(at < count, 0.0, DEAD)

    def far_bias(k):
        return jnp.concatenate([row_bias(first_position(2, fx, fc) + k * SUB, SUB) for fx, fc in KINDS], axis=0)

    def pairs(rows, bias, lowest, n):
        cols = slice(lowest * ROWS, (lowest + n) * ROWS)
        s = scores_of(rows, win[cols])
        best_win[:, cols] = jnp.maximum(best_win[:, cols], over_rows(add_rows_bias(s, bias)))
        return over_cols(s + live_cols[:, cols])

    def win_pairs(dz, lowest, n):
        own = slice(PLACE[dz] * ROWS, (PLACE[dz] + 1) * ROWS)
        best = pairs(win[own], row_bias(first_position(dz), ROWS), lowest, n)
        best_win[:, own] = jnp.maximum(best_win[:, own], turned(best))

    def far_pairs(k, lowest, n):
        best = pairs(far[k], far_bias(k), lowest, n)
        best_far_rows[k] = best if lowest == 0 else jnp.maximum(best_far_rows[k], best)

    def far_done(k):
        best = turned(best_far_rows[k])
        for kind in range(3):
            best_far[kind, :, k * SUB : (k + 1) * SUB] = best[:, kind * SUB : (kind + 1) * SUB]

    def large_self():
        own = slice(own_first, own_first + ROWS)
        s = scores_of(win[own], win[own])
        r = lax.broadcasted_iota(jnp.int32, s.shape, 0)
        q = lax.broadcasted_iota(jnp.int32, s.shape, 1)
        s = add_rows_bias(jnp.where(r == q, DEAD, s), row_bias(first_position(0), ROWS))
        best_win[:, own] = jnp.maximum(best_win[:, own], over_rows(s))

    def small_col_bias(meta_row, meta_col, first, n):
        at = first + lax.broadcasted_iota(jnp.int32, (1, n), 1)
        r = jnp.concatenate([meta_row[0:1]] * (n // 128), axis=1)
        q = jnp.concatenate([meta_col[0:1]] * (n // 128), axis=1)
        return jnp.where(((r >> 10) == (q >> 10)) & (at < (q & 1023)), 0.0, DEAD)

    def small_row_bias(meta_row, meta_col, first, n):
        at = first + lax.broadcasted_iota(jnp.int32, (n, 128), 0)
        r, q = meta_row[0:1], meta_col[0:1]
        live = jnp.where((r >> 10) == (q >> 10), r & 1023, 0)
        return jnp.where(at < live, 0.0, DEAD)

    def small_self():
        for f in range(0, BR, HALF):
            s = scores_of(near[1, f : f + HALF], near[1])
            r = f + lax.broadcasted_iota(jnp.int32, s.shape, 0)
            q = lax.broadcasted_iota(jnp.int32, s.shape, 1)
            bias = small_row_bias(meta[1], meta[1], f, HALF)
            s = add_rows_bias(jnp.where(r == q, DEAD, s), bias)
            best_near[1] = jnp.maximum(best_near[1], over_rows(s))

    def one_above():
        def step(h, carry):
            f = pl.multiple_of(h * HALF, HALF)
            s = scores_of(near[2, pl.ds(f, HALF)], near[1])
            rb = small_row_bias(meta[2], meta[1], f, HALF)
            cb = small_col_bias(meta[2], meta[1], 0, BR)
            best_near[1] = jnp.maximum(best_near[1], over_rows(add_rows_bias(s, rb)))
            best_near_rows[0, pl.ds(f, HALF)] = jnp.maximum(best_near_rows[0, pl.ds(f, HALF)], over_cols(s + cb))
            return carry

        lax.fori_loop(0, 2, step, 0)

    def two_apart():
        low = 1 - y // 2

        def step(h, carry):
            fr = pl.multiple_of((h * low + (1 - low)) * HALF, HALF)
            fc = pl.multiple_of(h * (1 - low) * HALF, HALF)
            s = scores_of(near[2, pl.ds(fr, HALF)], near[0, pl.ds(fc, HALF)])
            rb = small_row_bias(meta[2], meta[0], fr, HALF)
            cb = small_col_bias(meta[2], meta[0], fc, HALF)
            best_near[0, :, pl.ds(fc, HALF)] = jnp.maximum(
                best_near[0, :, pl.ds(fc, HALF)], over_rows(add_rows_bias(s, rb))
            )
            best_near_rows[0, pl.ds(fr, HALF)] = jnp.maximum(best_near_rows[0, pl.ds(fr, HALF)], over_cols(s + cb))
            return carry

        lax.fori_loop(0, 2, step, 0)

    def with_across(lowest, n):
        def step(j, carry):
            slot = lowest + j // 2
            f = pl.multiple_of(lax.rem(j, 2) * HALF, HALF)
            s = scores_of(across[pl.ds(f, HALF)], near[slot])
            rb = small_row_bias(meta_across[...], meta[slot], f, HALF)
            cb = small_col_bias(meta_across[...], meta[slot], 0, BR)
            best_near[slot] = jnp.maximum(best_near[slot], over_rows(add_rows_bias(s, rb)))
            best_near_rows[1, pl.ds(f, HALF)] = jnp.maximum(best_near_rows[1, pl.ds(f, HALF)], over_cols(s + cb))
            return carry

        lax.fori_loop(0, 2 * n, step, 0)

    def take(k):
        fwd_copy(1, k).wait_recv()
        cross_copy(k).start()
        sib_copy(k).start()

    def pass_on(k):
        cross_copy(k).wait_recv()
        diag_copy(k).start()

    def arrived(k):
        sib_copy(k).wait_recv()
        diag_copy(k).wait_recv()

    large_self()
    small_self()
    ends = [first + n for first, n in PIECES]
    halves_due = next(k for k in range(N_PIECE) if ends[k] >= 2 * SUB)
    for k in range(N_PIECE):
        for i in range(2):
            own_copy(i, k).wait_recv()
            if k == 0:
                first = PLACE[2 * i - 1] * ROWS
                piece = slice(first, first + PIECES[0][1])
                win[piece] = unit_rows(win[piece])
            fwd_copy(i, k).start()
        if k == halves_due:
            for i in range(2):
                near_copy(i, 0).wait_recv()
            for n in range(3):
                meta_copy(n).wait_recv()

            @pl.when(wide)
            def _():
                for i in range(2):
                    hop_copy(i).start()
                meta_copy(3).start()
                across_copy().wait_recv()
                with_across(1, 1)

    win_pairs(1, 1, 2)

    def small_first():
        for i in range(2):
            near_copy(i, 1).wait_recv()
        one_above()
        two_apart()

        @pl.when(wide)
        def _():
            with_across(0, 1)
            with_across(2, 1)

    def small_last():
        @pl.when(wide)
        def _():
            for i in range(2):
                hop_copy(i).wait_recv()
            meta_copy(3).wait_recv()
            with_across(3, 1)
            best_across[...] = turned(best_near_rows[1])

        best_near[2] = jnp.maximum(best_near[2], turned(best_near_rows[0]))
        for n in range(2):
            small_result(n).start()

        @pl.when(wide)
        def _():
            for n in (2, 3):
                small_result(n).start()

    seen = passed = 0
    for k in range(N_PIECE):
        take(k)
        if ends[k] <= 2 * SUB:
            while passed < k:
                pass_on(passed)
                passed += 1
        if ends[k] == SUB:
            small_first()
        if ends[k] == 2 * SUB:
            small_last()
        while seen < passed - 1:
            arrived(seen)
            seen += 1
            if ends[seen - 1] % SUB == 0:
                far_pairs(ends[seen - 1] // SUB - 1, 0, 3)
    while ends[passed] < ROWS:
        pass_on(passed)
        passed += 1
    while ends[seen] <= 2 * SUB:
        arrived(seen)
        seen += 1
        if ends[seen - 1] % SUB == 0:
            far_pairs(ends[seen - 1] // SUB - 1, 0, 3)
    for k in range(N_PIECE):
        fwd_copy(0, k).wait_recv()
    win_pairs(2, 2, 2)
    far_pairs(0, 3, 2)
    far_done(0)
    pass_on(N_PIECE - 1)
    far_pairs(1, 3, 2)
    far_done(1)
    for k in range(seen, N_PIECE):
        arrived(k)
    far_pairs(2, 0, 5)
    far_done(2)
    for n in range(7):
        large_result(n).start()

    at = lax.broadcasted_iota(jnp.int32, (1, BR), 1)
    for n in range(3):
        small_result(n).wait_recv()
    best = best_near[1]
    for n in range(3):
        best = jnp.maximum(best, got_small[n])
    small_out[...] = jnp.where(at < small_count[0, 0], jnp.max(best, axis=0, keepdims=True), 0.0)
    for k in range(N_PIECE):
        for i in range(2):
            own_copy(i, k).wait_send()
            fwd_copy(i, k).wait_send()
        sib_copy(k).wait_send()
        cross_copy(k).wait_send()
        diag_copy(k).wait_send()
    for i in range(2):
        for h in range(2):
            near_copy(i, h).wait_send()
    for n in range(3):
        meta_copy(n).wait_send()
    for n in range(2):
        small_result(n).wait_send()

    @pl.when(wide)
    def _():
        for i in range(2):
            hop_copy(i).wait_send()
        meta_copy(3).wait_send()
        for n in (2, 3):
            small_result(n).wait_send()

    @pl.when(thin)
    def _():
        across_copy().wait_send()

    at = first_position(0) + lax.broadcasted_iota(jnp.int32, (1, ROWS), 1)
    for n in range(7):
        large_result(n).wait_recv()
    best = best_win[:, own_first : own_first + ROWS]
    for n in range(7):
        best = jnp.maximum(best, got_large[n])
    large_out[...] = jnp.where(at < count, jnp.max(best, axis=0, keepdims=True), 0.0)
    for n in range(7):
        large_result(n).wait_send()


def hand_out(large, small, large_out, small_out):
    large_out[...] = large[...].reshape(ROWS)
    small_out[...] = small[...].reshape(1, 1, BR)


def body(large_emb, large_count, small_emb, small_ids, small_count):
    vmem = pl.BlockSpec(memory_space=pltpu.VMEM)
    dma = pltpu.SemaphoreType.DMA
    f32, bf16, i32 = jnp.float32, jnp.bfloat16, jnp.int32
    large, small = pl.pallas_call(
        kernel,
        out_shape=(jax.ShapeDtypeStruct((1, ROWS), f32), jax.ShapeDtypeStruct((1, BR), f32)),
        in_specs=[pl.BlockSpec(memory_space=pl.ANY)] * 5,
        out_specs=(vmem, vmem),
        scratch_shapes=[
            pltpu.VMEM((ROWS, D), bf16),
            pltpu.VMEM((BR, D), bf16),
            pltpu.VMEM((5 * ROWS, D), bf16),
            pltpu.VMEM((ROWS // SUB, 3 * SUB, D), bf16),
            pltpu.VMEM((4, BR, D), bf16),
            pltpu.VMEM((BR, D), bf16),
            pltpu.VMEM((4, 8, 128), i32),
            pltpu.VMEM((8, 128), i32),
            pltpu.VMEM((1, 5 * ROWS), f32),
            pltpu.VMEM((8, 5 * ROWS), f32),
            pltpu.VMEM((ROWS // SUB, 3 * SUB, 128), f32),
            pltpu.VMEM((3, 8, ROWS), f32),
            pltpu.VMEM((4, 8, BR), f32),
            pltpu.VMEM((2, BR, 128), f32),
            pltpu.VMEM((8, BR), f32),
            pltpu.VMEM((7, 8, ROWS), f32),
            pltpu.VMEM((3, 8, BR), f32),
            pltpu.SMEM((1,), i32), pltpu.SMEM((1, 1), i32), pltpu.SMEM((1, 1), i32),
            dma((3,)), dma((3,)), dma((2, N_PIECE)), dma((2, N_PIECE)), dma((2, N_PIECE)), dma((2, N_PIECE)),
            dma((N_PIECE,)), dma((N_PIECE,)), dma((N_PIECE,)), dma((N_PIECE,)), dma((N_PIECE,)), dma((N_PIECE,)),
            dma((2, 2)), dma((2, 2)), dma((2,)), dma((2,)), dma((1,)), dma((1,)), dma((4,)), dma((4,)),
            dma((7,)), dma((7,)), dma((4,)), dma((3,)),
        ],
        compiler_params=pltpu.CompilerParams(
            collective_id=0, has_side_effects=True, vmem_limit_bytes=63_200_000
        ),
        name="cluster_maxima",
    )(large_count, small_ids, small_count, large_emb, small_emb.reshape(BR, D))
    return pl.pallas_call(
        hand_out,
        out_shape=(jax.ShapeDtypeStruct((ROWS,), f32), jax.ShapeDtypeStruct((1, 1, BR), f32)),
        in_specs=[vmem, vmem],
        out_specs=(vmem, vmem),
        name="hand_out",
    )(large, small)


def solution(mesh):
    placed = (
        P(("grp", "blk"), None),
        P("grp"),
        P("grp", "blk", None, None),
        P("grp", "blk"),
        P("grp", "blk"),
    )
    return jax.shard_map(
        body,
        mesh=mesh,
        in_specs=placed,
        out_specs=(P(("grp", "blk")), P("grp", "blk", None)),
        check_vma=False,
    )
```

time: 59.4 us -> 55.1 us (0.928)
  local copies, waits for them, and re-layouts: 2.77 us -> 0 us
  Pallas kernels: 53.3 us -> 52.4 us
  other arithmetic: 0.6 us -> 0 us
    unnamed x5 -> x0, local copies, waits for them, and re-layouts: 2.77 us -> none
    pallas_call x1, Pallas kernels: 53.3 us -> 51.1 us  [body(): pl.pallas_call(kernel, out_shape=(jax.ShapeDtypeStruct((1, ROWS), f32), j...]
    pallas_call x0 -> x1, Pallas kernels: none -> 1.26 us  [body(): pl.pallas_call(hand_out, out_shape=(jax.ShapeDtypeStruct((ROWS,), f32), j...]
    pallas_call x1 -> x0, other arithmetic: 0.6 us -> none  [body(): pl.pallas_call(kernel, out_shape=(jax.ShapeDtypeStruct((1, ROWS), f32), j...]
where the time goes in v2:
time: 55.1 us; the launch traced here: 55 us
  Pallas kernels  52.4 us (95%)
  between operations  2.58 us (5%)
    pallas_call x1, Pallas kernels, body(): pl.pallas_call(kernel, out_shape=(jax.ShapeDtypeStruct((1, ROWS), f32), j...  51.1 us
    pallas_call x1, Pallas kernels, body(): pl.pallas_call(hand_out, out_shape=(jax.ShapeDtypeStruct((ROWS,), f32), j...  1.26 us

profile of v2, /device:TPU:1, one launch (start us, length us, event | category | flops | bytes accessed | tf_op | source)
XLA Modules:
  0.0 55.0 jit_solution(11516984966716243533)
XLA Ops:
  2.6 51.1 %cluster_maxima.1 = (f32[1,384]{1,0:T(1,128)}, f32[1,512]{1,0:T(1,128)}) custom-call(s32[1]{0:T(128)S(6)} %copy.7.large_count_in, s32[1,1]{1,0:T(1,128)S(6)} %copy.8.small_id_in, s32[1,1]{1,0:T(1,128)S(6)} %copy.9.small_count_in, bf16[384,768]{1,0:T(8,128)(2,1)} %large_emb.1, bf16[512,768]{1,0:T(8,128)(2,1)} %bitcast.1), custom_call_target="tpu_custom_call" | custom-call | tf_op jit(solution)/shard_map/cluster_maxima/pallas_call | solution.py:468
  53.7 1.3 %hand_out.1 = (f32[384]{0:T(512)}, f32[1,1,512]{2,1,0:T(1,128)}) custom-call(f32[1,384]{1,0:T(1,128)} %get-tuple-element.4.large, f32[1,512]{1,0:T(1,128)} %get-tuple-element.5.small), custom_call_target="tpu_custom_call" | custom-call | tf_op jit(solution)/shard_map/hand_out/pallas_call | solution.py:502

commit v3 on v2

--- a/solution.py
+++ b/solution.py
@@ -383,7 +383,7 @@
             small_first()
         if ends[k] == 2 * SUB:
             small_last()
-        while seen < passed - 1:
+        while seen < passed - 2:
             arrived(seen)
             seen += 1
             if ends[seen - 1] % SUB == 0:
@@ -407,8 +407,10 @@
     for k in range(seen, N_PIECE):
         arrived(k)
     far_pairs(2, 0, 5)
+    for n in (0, 3, 1, 2):
+        large_result(n).start()
     far_done(2)
-    for n in range(7):
+    for n in (6, 5, 4):
         large_result(n).start()
 
     at = lax.broadcasted_iota(jnp.int32, (1, BR), 1)

time: 55.1 us -> 55.1 us (level)
  no operation moved by 1% of the time
where the time goes in v3:
time: 55.1 us; the launch traced here: 55 us
  Pallas kernels  52.4 us (95%)
  between operations  2.58 us (5%)
    pallas_call x1, Pallas kernels, body(): pl.pallas_call(kernel, out_shape=(jax.ShapeDtypeStruct((1, ROWS), f32), j...  51.1 us
    pallas_call x1, Pallas kernels, body(): pl.pallas_call(hand_out, out_shape=(jax.ShapeDtypeStruct((ROWS,), f32), j...  1.26 us

profile of v3, /device:TPU:1, one launch (start us, length us, event | category | flops | bytes accessed | tf_op | source)
XLA Modules:
  0.0 55.0 jit_solution(9167533233839664749)
XLA Ops:
  2.6 51.1 %cluster_maxima.1 = (f32[1,384]{1,0:T(1,128)}, f32[1,512]{1,0:T(1,128)}) custom-call(s32[1]{0:T(128)S(6)} %copy.7.large_count_in, s32[1,1]{1,0:T(1,128)S(6)} %copy.8.small_id_in, s32[1,1]{1,0:T(1,128)S(6)} %copy.9.small_count_in, bf16[384,768]{1,0:T(8,128)(2,1)} %large_emb.1, bf16[512,768]{1,0:T(8,128)(2,1)} %bitcast.1), custom_call_target="tpu_custom_call" | custom-call | tf_op jit(solution)/shard_map/cluster_maxima/pallas_call | solution.py:470
  53.7 1.3 %hand_out.1 = (f32[384]{0:T(512)}, f32[1,1,512]{2,1,0:T(1,128)}) custom-call(f32[1,384]{1,0:T(1,128)} %get-tuple-element.4.large, f32[1,512]{1,0:T(1,128)} %get-tuple-element.5.small), custom_call_target="tpu_custom_call" | custom-call | tf_op jit(solution)/shard_map/hand_out/pallas_call | solution.py:504

commit v4 on v2

--- a/solution.py
+++ b/solution.py
@@ -396,19 +396,19 @@
         seen += 1
         if ends[seen - 1] % SUB == 0:
             far_pairs(ends[seen - 1] // SUB - 1, 0, 3)
+    pass_on(N_PIECE - 1)
     for k in range(N_PIECE):
         fwd_copy(0, k).wait_recv()
     win_pairs(2, 2, 2)
     far_pairs(0, 3, 2)
     far_done(0)
-    pass_on(N_PIECE - 1)
     far_pairs(1, 3, 2)
     far_done(1)
     for k in range(seen, N_PIECE):
         arrived(k)
     far_pairs(2, 0, 5)
     far_done(2)
-    for n in range(7):
+    for n in (6, 5, 4, 0, 3, 1, 2):
         large_result(n).start()
 
     at = lax.broadcasted_iota(jnp.int32, (1, BR), 1)

time: 55.1 us -> 54.9 us (level)
  no operation moved by 1% of the time
where the time goes in v4:
time: 54.9 us; the launch traced here: 54.8 us
  Pallas kernels  52.2 us (95%)
  between operations  2.58 us (5%)
    pallas_call x1, Pallas kernels, body(): pl.pallas_call(kernel, out_shape=(jax.ShapeDtypeStruct((1, ROWS), f32), j...  50.9 us
    pallas_call x1, Pallas kernels, body(): pl.pallas_call(hand_out, out_shape=(jax.ShapeDtypeStruct((ROWS,), f32), j...  1.26 us

profile of v4, /device:TPU:1, one launch (start us, length us, event | category | flops | bytes accessed | tf_op | source)
XLA Modules:
  0.0 54.8 jit_solution(12767063426361580918)
XLA Ops:
  2.6 50.9 %cluster_maxima.1 = (f32[1,384]{1,0:T(1,128)}, f32[1,512]{1,0:T(1,128)}) custom-call(s32[1]{0:T(128)S(6)} %copy.7.large_count_in, s32[1,1]{1,0:T(1,128)S(6)} %copy.8.small_id_in, s32[1,1]{1,0:T(1,128)S(6)} %copy.9.small_count_in, bf16[384,768]{1,0:T(8,128)(2,1)} %large_emb.1, bf16[512,768]{1,0:T(8,128)(2,1)} %bitcast.1), custom_call_target="tpu_custom_call" | custom-call | tf_op jit(solution)/shard_map/cluster_maxima/pallas_call | solution.py:468
  53.5 1.3 %hand_out.1 = (f32[384]{0:T(512)}, f32[1,1,512]{2,1,0:T(1,128)}) custom-call(f32[1,384]{1,0:T(1,128)} %get-tuple-element.4.large, f32[1,512]{1,0:T(1,128)} %get-tuple-element.5.small), custom_call_target="tpu_custom_call" | custom-call | tf_op jit(solution)/shard_map/hand_out/pallas_call | solution.py:502
